TPU v7x, 32 devices: a whole 2x2x4 slice. The times are simulated.
32 devices in a mesh: row: 4 (over y, core), col: 8 (over z, x).
Axes of the slice: x: 2, y: 2, z: 4, core: 2. Of those that a mesh axis runs over, the one named last changes fastest.
Arguments:
- cotangent: bfloat16 [8, 128, 16384], P(None, 'row', 'col'), may hold values from -6 to 6
- pre_act: bfloat16 [8, 128, 16384], P(None, 'row', 'col'), may hold values from -6 to 6
- kernel_one: bfloat16 [576, 64], replicated, may hold values from -0.25 to 0.25
- kernel_two: bfloat16 [576, 64], replicated, may hold values from -0.25 to 0.25
- offsets: int32 [2, 8, 128, 256], P(None, None, 'row', 'col'), may hold values from 0 to 62, as said below
- fractions: int32 [2, 8, 128, 256], P(None, None, 'row', 'col'), may hold values from 0 to 15
- anchors: int32 [2, 8, 4, 8], P(None, None, 'row', 'col'), may hold values from -1 to 0
Outputs:
- grad_ref: float32 [8, 128, 16384], P(None, 'row', 'col')
Inputs may be any that keep to these rules, and one draw needn't show every extreme that they name: offsets index rows and columns of the (64) x (64) region of a tile.
All inputs are finite; a program needn't handle non-finite values.
Results may differ from a plain program's by a relative error of at most 0.0044.
Values may be sent and summed in bfloat16 or wider, within the bound.
A program may use at most 128 MiB of HBM per device.

v0:
```python
import jax
import jax.numpy as jnp
from jax import lax
from jax.sharding import PartitionSpec as P


def extended(x, sides, width):
    for axis, dim in sides:
        peers, length = (lax.axis_size(axis), x.shape[dim])
        up = [(i, (i + 1) % peers) for i in range(peers - 1)]
        down = [(j, i) for i, j in up]
        last = lax.slice_in_dim(x, length - width, length, axis=dim)
        initial = lax.slice_in_dim(x, 0, width, axis=dim)
        before = lax.ppermute(last, axis, up)
        after = lax.ppermute(initial, axis, down)
        x = jnp.concatenate([before, x, after], axis=dim)
    return x


def passed_along(x, axis, by):
    peers = lax.axis_size(axis)
    pairs = [(i, i + by) for i in range(peers) if 0 <= i + by < peers]
    return lax.ppermute(x, axis, pairs)


def stacked_kernel(kernel, channels):
    return jnp.concatenate(
        [
            kernel[(3 * shift_y + shift_x) * channels : (3 * shift_y + shift_x + 1) * channels].T
            for shift_y in range(3)
            for shift_x in range(3)
        ],
        axis=0,
    )


def conv_back(padded, kernel_stack, rows_out, cols_out):
    patches = jnp.concatenate(
        [
            padded[:, 2 - shift_y : 2 - shift_y + rows_out, 2 - shift_x : 2 - shift_x + cols_out, :]
            for shift_y in range(3)
            for shift_x in range(3)
        ],
        axis=-1,
    )
    return jnp.einsum("fyxk,kc->fyxc", patches, kernel_stack, preferred_element_type=jnp.float32)


def frame_region(frame_items):
    warped_frame, offset_frame, fraction_frame = frame_items
    tile_h, tile_w, channels = warped_frame.shape
    pixels = tile_h * tile_w
    region_h = 2 * tile_h
    region_w = 2 * tile_w
    values = warped_frame.reshape(pixels, channels)
    row_start = offset_frame[0].reshape(pixels, 1)
    col_start = offset_frame[1].reshape(pixels, 1)
    frac_y = fraction_frame[0].reshape(pixels, 1).astype(jnp.float32) / 16.0
    frac_x = fraction_frame[1].reshape(pixels, 1).astype(jnp.float32) / 16.0
    row_span = lax.broadcasted_iota(jnp.int32, (pixels, region_h), 1)
    col_span = lax.broadcasted_iota(jnp.int32, (pixels, region_w), 1)
    row_weight = jnp.where(row_span == row_start, 1.0 - frac_y, 0.0) + jnp.where(
        row_span == row_start + 1, frac_y, 0.0
    )
    total = jnp.zeros((region_h, region_w * channels), jnp.float32)
    for corner_x in range(2):
        weight_x = frac_x if corner_x == 1 else 1.0 - frac_x
        spread_weight = (row_weight * weight_x).astype(jnp.bfloat16)
        onehot = (col_span == col_start + corner_x).astype(jnp.bfloat16)
        spread = (onehot[:, :, None] * values[:, None, :]).reshape(pixels, region_w * channels)
        total = total + lax.dot_general(
            spread_weight, spread, (((0,), (0,)), ((), ())), preferred_element_type=jnp.float32
        )
    region = total.reshape(2, tile_h, 2, tile_w * channels)
    return jnp.transpose(region, (0, 2, 1, 3)).astype(jnp.bfloat16)


def bilinear_back(warped, offsets, fractions):
    offset_frames = jnp.transpose(offsets, (1, 0, 2, 3))
    fraction_frames = jnp.transpose(fractions, (1, 0, 2, 3))
    regions = lax.map(frame_region, (warped, offset_frames, fraction_frames))
    return jnp.transpose(regions, (1, 2, 0, 3, 4))


def frame_mask(cond, dtype):
    return cond.astype(dtype)[:, None, None]


def section_split(pieces, anchor):
    first_half = pieces[0]
    second_half = pieces[1]
    going_low = frame_mask(anchor == -1, jnp.bfloat16)
    going_high = frame_mask(anchor == 0, jnp.bfloat16)
    lower_part = first_half * going_low
    upper_part = second_half * going_high
    staying = first_half * going_high + second_half * going_low
    return (lower_part, upper_part, staying)


def section_merge(sets):
    to_lower = 0.0
    to_upper = 0.0
    remain = 0.0
    for part_set, other_anchor in sets:
        low_mask = frame_mask(other_anchor == -1, jnp.float32)
        high_mask = frame_mask(other_anchor == 0, jnp.float32)
        to_lower = to_lower + part_set[0].astype(jnp.float32) * low_mask
        to_upper = to_upper + part_set[1].astype(jnp.float32) * high_mask
        remain = (
            remain
            + part_set[0].astype(jnp.float32) * high_mask
            + part_set[1].astype(jnp.float32) * low_mask
        )
    return (to_lower, to_upper, remain)


def shards(cotangent, pre_act, kernel_one, kernel_two, offsets, fractions, anchors):
    frames, tile_h, width_c = cotangent.shape
    channels = kernel_one.shape[1]
    tile_w = width_c // channels
    grad_grid = cotangent.reshape(frames, tile_h, tile_w, channels)
    pre_grid = pre_act.reshape(frames, tile_h, tile_w, channels)
    first_stack = stacked_kernel(kernel_one, channels)
    second_stack = stacked_kernel(kernel_two, channels)
    grad_padded = extended(grad_grid, (("row", 1), ("col", 2)), 1)
    hidden_grad = (
        conv_back(grad_padded, second_stack, tile_h, tile_w) * (pre_grid > 0).astype(jnp.float32)
    ).astype(jnp.bfloat16)
    hidden_padded = extended(hidden_grad, (("row", 1), ("col", 2)), 1)
    warped = (
        grad_grid.astype(jnp.float32) + conv_back(hidden_padded, first_stack, tile_h, tile_w)
    ).astype(jnp.bfloat16)
    pieces = bilinear_back(warped, offsets, fractions)
    row_anchor = anchors[0, :, 0, 0]
    col_anchor = anchors[1, :, 0, 0]
    lower_part, upper_part, staying = section_split(pieces, row_anchor)
    own_other = col_anchor.astype(jnp.bfloat16)
    got_lower, lower_other = passed_along((lower_part, own_other), "row", -1)
    got_upper, upper_other = passed_along((upper_part, own_other), "row", 1)
    to_lower, to_upper, remain = section_merge(
        ((staying, own_other), (got_lower, lower_other), (got_upper, upper_other))
    )
    summed = remain + passed_along(to_lower, "col", -1) + passed_along(to_upper, "col", 1)
    return summed


def solution(mesh):
    in_specs = (
        P(None, "row", "col"),
        P(None, "row", "col"),
        P(),
        P(),
        P(None, None, "row", "col"),
        P(None, None, "row", "col"),
        P(None, None, "row", "col"),
    )
    out_specs = P(None, "row", "col")
    return jax.shard_map(shards, mesh=mesh, in_specs=in_specs, out_specs=out_specs, check_vma=False)
```

profile of v0, /device:TPU:19, one launch (start us, length us, event | category | flops | bytes accessed | tf_op | source)
XLA Modules:
  0.0 402.6 jit_solution(5644026009644824425)
XLA Ops:
  33.9 11.8 %pad_maximum_fusion.3 = (bf16[8,32,32,64]{3,2,1,0:T(8,128)(2,1)}, bf16[8,32,32,64]{3,2,1,0:T(8,128)(2,1)}, bf16[8,32,32,64]{3,2,1,0:T(8,128)(2,1)}, bf16[8,32,32...) fusion(bf16[8,34,32,64]{3,2,1,0:T(8,128)(2,1)} %copy-done.2, ...), kind=kLoop, calls=%fused_computation.83 | loop fusion | flops 12582912 | bytes 7475200 | tf_op jit(solution)/shard_map/concatenate | solution.py:16
  45.8 21.9 %concatenate.57 = bf16[8,32,32,576]{3,2,1,0:T(8,128)(2,1)} concatenate(bf16[8,32,32,64]{3,2,1,0:T(8,128)(2,1)} %get-tuple-element.80, bf16[8,32,32,64]{3,2,1,0:T(8,128)(2,1)} %get-tuple-element.89, bf16[8,32,32,64]{3,2,1,0:T(8,128)(2,1)} %get-tuple-element.70, bf16[8,32,32,64]{3,2,1,0:T(8,128)(2,1)} %get-tuple-element.79, bf16[8,32,32,64]{3,2,1,0:T(8,128)(2,1)S(1)} %reshape.148, ...), dimensions={3} | concatenate | bytes 18874368 | tf_op jit(solution)/shard_map/concatenate | solution.py:38
  67.7 6.9 %select_convert_fusion = bf16[8,32,32,64]{3,2,1,0:T(8,128)(2,1)S(1)} fusion(pred[8,32,32,64]{3,2,1,0:T(32,128)(4,1)S(1)} %gt.11, bf16[8,32,32,576]{3,2,1,0:T(8,128)(2,1)} %concatenate.57, bf16[576,64]{0,1:T(8,128)(2,1)S(1)} %concatenate.58), kind=kOutput, calls=%fused_computation.41 | convolution fusion | flops 605028352 | bytes 11083776 | tf_op jit(solution)/shard_map/fyxk,kc->fyxc/dot_general | solution.py:46
  105.6 21.9 %concatenate.64 = bf16[8,32,32,576]{3,2,1,0:T(8,128)(2,1)} concatenate(bf16[8,32,32,64]{3,2,1,0:T(8,128)(2,1)} %get-tuple-element.68, bf16[8,32,32,64]{3,2,1,0:T(8,128)(2,1)} %get-tuple-element.85, bf16[8,32,32,64]{3,2,1,0:T(8,128)(2,1)} %get-tuple-element.65, bf16[8,32,32,64]{3,2,1,0:T(8,128)(2,1)} %get-tuple-element.67, bf16[8,32,32,64]{3,2,1,0:T(8,128)(2,1)S(1)} %select_convert_fusion, ...), dimensions={3} | concatenate | bytes 18874368 | tf_op jit(solution)/shard_map/concatenate | solution.py:38
  127.5 7.5 %add_convert_fusion = bf16[8,32,32,64]{3,2,1,0:T(8,128)(2,1)S(1)} fusion(bf16[8,32,32,64]{3,2,1,0:T(8,128)(2,1)} %copy-done.1, bf16[8,32,32,576]{3,2,1,0:T(8,128)(2,1)} %concatenate.64, bf16[576,64]{0,1:T(8,128)(2,1)S(1)} %concatenate.65), kind=kOutput, calls=%fused_computation.40 | convolution fusion | flops 605552640 | bytes 11608064 | tf_op jit(solution)/shard_map/fyxk,kc->fyxc/dot_general | solution.py:46
  135.0 154.0 %while.10 = (s32[]{:T(128)}, bf16[8,2,2,32,2048]{4,3,0,2,1:T(8,128)(2,1)}, s32[8,2,32,32]{3,2,1,0:T(8,128)}, s32[8,2,32,32]{3,2,1,0:T(8,128)S(1)}, bf16[8,32,32,...) while((s32[]{:T(128)}, bf16[8,2,2,32,2048]{4,3,0,2,1:T(8,128)(2,1)}, s32[8,2,32,32]{3,2,1,0:T(8,128)}, ...), condition=%wide.region_1.2_spmd, body=%wide.region_0.1_spmd.sunk | while | flops 1083842560 | bytes 73155216 | solution.py:81
  136.3 6.9 %broadcast_multiply_fusion.3 = (bf16[1024,64,64]{0,2,1:T(8,128)(2,1)}, bf16[1024,64,64]{0,2,1:T(8,128)(2,1)}) fusion(bf16[1024,64]{0,1:T(8,128)(2,1)S(1)} %get-tuple-element.163, bf16[1024,64]{0,1:T(8,128)(2,1)S(1)} %copy.101, bf16[1024,64]{0,1:T(8,128)(2,1)S(1)} %get-tuple-element.164), kind=kLoop, calls=%fused_computation.2.clone.1 | loop fusion | flops 8388608 | bytes 17170432 | tf_op jit(solution)/shard_map/while/body/eval_jaxpr/mul | solution.py:70
  143.4 6.2 %fusion.63 = f32[64,4096]{1,0:T(8,128)S(1)} fusion(bf16[1024,4096]{0,1:T(8,128)(2,1)} %bitcast.128, f32[1024]{0:T(1024)S(1)} %get-tuple-element.168, f32[1024]{0:T(1024)S(1)} %div.17, s32[1024]{0:T(1024)S(1)} %broadcast_add_fusion.5, f32[1024]{0:T(1024)S(1)} %get-tuple-element.170, s32[1024]{0:T(1024)S(1)} %eq.159), kind=kOutput, calls=%fused_computation.10.clone.1 | convolution fusion | flops 537329664 | bytes 9457664 | tf_op jit(solution)/shard_map/while/body/eval_jaxpr/dot_general | solution.py:71
  155.5 6.9 %broadcast_multiply_fusion.3 = (bf16[1024,64,64]{0,2,1:T(8,128)(2,1)}, bf16[1024,64,64]{0,2,1:T(8,128)(2,1)}) fusion(bf16[1024,64]{0,1:T(8,128)(2,1)S(1)} %get-tuple-element.163, bf16[1024,64]{0,1:T(8,128)(2,1)S(1)} %copy.101, bf16[1024,64]{0,1:T(8,128)(2,1)S(1)} %get-tuple-element.164), kind=kLoop, calls=%fused_computation.2.clone.1 | loop fusion | flops 8388608 | bytes 17170432 | tf_op jit(solution)/shard_map/while/body/eval_jaxpr/mul | solution.py:70
  162.6 6.2 %fusion.63 = f32[64,4096]{1,0:T(8,128)S(1)} fusion(bf16[1024,4096]{0,1:T(8,128)(2,1)} %bitcast.128, f32[1024]{0:T(1024)S(1)} %get-tuple-element.168, f32[1024]{0:T(1024)S(1)} %div.17, s32[1024]{0:T(1024)S(1)} %broadcast_add_fusion.5, f32[1024]{0:T(1024)S(1)} %get-tuple-element.170, s32[1024]{0:T(1024)S(1)} %eq.159), kind=kOutput, calls=%fused_computation.10.clone.1 | convolution fusion | flops 537329664 | bytes 9457664 | tf_op jit(solution)/shard_map/while/body/eval_jaxpr/dot_general | solution.py:71
  174.7 6.9 %broadcast_multiply_fusion.3 = (bf16[1024,64,64]{0,2,1:T(8,128)(2,1)}, bf16[1024,64,64]{0,2,1:T(8,128)(2,1)}) fusion(bf16[1024,64]{0,1:T(8,128)(2,1)S(1)} %get-tuple-element.163, bf16[1024,64]{0,1:T(8,128)(2,1)S(1)} %copy.101, bf16[1024,64]{0,1:T(8,128)(2,1)S(1)} %get-tuple-element.164), kind=kLoop, calls=%fused_computation.2.clone.1 | loop fusion | flops 8388608 | bytes 17170432 | tf_op jit(solution)/shard_map/while/body/eval_jaxpr/mul | solution.py:70
  181.8 6.2 %fusion.63 = f32[64,4096]{1,0:T(8,128)S(1)} fusion(bf16[1024,4096]{0,1:T(8,128)(2,1)} %bitcast.128, f32[1024]{0:T(1024)S(1)} %get-tuple-element.168, f32[1024]{0:T(1024)S(1)} %div.17, s32[1024]{0:T(1024)S(1)} %broadcast_add_fusion.5, f32[1024]{0:T(1024)S(1)} %get-tuple-element.170, s32[1024]{0:T(1024)S(1)} %eq.159), kind=kOutput, calls=%fused_computation.10.clone.1 | convolution fusion | flops 537329664 | bytes 9457664 | tf_op jit(solution)/shard_map/while/body/eval_jaxpr/dot_general | solution.py:71
  193.9 6.9 %broadcast_multiply_fusion.3 = (bf16[1024,64,64]{0,2,1:T(8,128)(2,1)}, bf16[1024,64,64]{0,2,1:T(8,128)(2,1)}) fusion(bf16[1024,64]{0,1:T(8,128)(2,1)S(1)} %get-tuple-element.163, bf16[1024,64]{0,1:T(8,128)(2,1)S(1)} %copy.101, bf16[1024,64]{0,1:T(8,128)(2,1)S(1)} %get-tuple-element.164), kind=kLoop, calls=%fused_computation.2.clone.1 | loop fusion | flops 8388608 | bytes 17170432 | tf_op jit(solution)/shard_map/while/body/eval_jaxpr/mul | solution.py:70
  201.1 6.2 %fusion.63 = f32[64,4096]{1,0:T(8,128)S(1)} fusion(bf16[1024,4096]{0,1:T(8,128)(2,1)} %bitcast.128, f32[1024]{0:T(1024)S(1)} %get-tuple-element.168, f32[1024]{0:T(1024)S(1)} %div.17, s32[1024]{0:T(1024)S(1)} %broadcast_add_fusion.5, f32[1024]{0:T(1024)S(1)} %get-tuple-element.170, s32[1024]{0:T(1024)S(1)} %eq.159), kind=kOutput, calls=%fused_computation.10.clone.1 | convolution fusion | flops 537329664 | bytes 9457664 | tf_op jit(solution)/shard_map/while/body/eval_jaxpr/dot_general | solution.py:71
  213.2 6.9 %broadcast_multiply_fusion.3 = (bf16[1024,64,64]{0,2,1:T(8,128)(2,1)}, bf16[1024,64,64]{0,2,1:T(8,128)(2,1)}) fusion(bf16[1024,64]{0,1:T(8,128)(2,1)S(1)} %get-tuple-element.163, bf16[1024,64]{0,1:T(8,128)(2,1)S(1)} %copy.101, bf16[1024,64]{0,1:T(8,128)(2,1)S(1)} %get-tuple-element.164), kind=kLoop, calls=%fused_computation.2.clone.1 | loop fusion | flops 8388608 | bytes 17170432 | tf_op jit(solution)/shard_map/while/body/eval_jaxpr/mul | solution.py:70
  220.3 6.2 %fusion.63 = f32[64,4096]{1,0:T(8,128)S(1)} fusion(bf16[1024,4096]{0,1:T(8,128)(2,1)} %bitcast.128, f32[1024]{0:T(1024)S(1)} %get-tuple-element.168, f32[1024]{0:T(1024)S(1)} %div.17, s32[1024]{0:T(1024)S(1)} %broadcast_add_fusion.5, f32[1024]{0:T(1024)S(1)} %get-tuple-element.170, s32[1024]{0:T(1024)S(1)} %eq.159), kind=kOutput, calls=%fused_computation.10.clone.1 | convolution fusion | flops 537329664 | bytes 9457664 | tf_op jit(solution)/shard_map/while/body/eval_jaxpr/dot_general | solution.py:71
  232.4 6.9 %broadcast_multiply_fusion.3 = (bf16[1024,64,64]{0,2,1:T(8,128)(2,1)}, bf16[1024,64,64]{0,2,1:T(8,128)(2,1)}) fusion(bf16[1024,64]{0,1:T(8,128)(2,1)S(1)} %get-tuple-element.163, bf16[1024,64]{0,1:T(8,128)(2,1)S(1)} %copy.101, bf16[1024,64]{0,1:T(8,128)(2,1)S(1)} %get-tuple-element.164), kind=kLoop, calls=%fused_computation.2.clone.1 | loop fusion | flops 8388608 | bytes 17170432 | tf_op jit(solution)/shard_map/while/body/eval_jaxpr/mul | solution.py:70
  239.5 6.2 %fusion.63 = f32[64,4096]{1,0:T(8,128)S(1)} fusion(bf16[1024,4096]{0,1:T(8,128)(2,1)} %bitcast.128, f32[1024]{0:T(1024)S(1)} %get-tuple-element.168, f32[1024]{0:T(1024)S(1)} %div.17, s32[1024]{0:T(1024)S(1)} %broadcast_add_fusion.5, f32[1024]{0:T(1024)S(1)} %get-tuple-element.170, s32[1024]{0:T(1024)S(1)} %eq.159), kind=kOutput, calls=%fused_computation.10.clone.1 | convolution fusion | flops 537329664 | bytes 9457664 | tf_op jit(solution)/shard_map/while/body/eval_jaxpr/dot_general | solution.py:71
  251.6 6.9 %broadcast_multiply_fusion.3 = (bf16[1024,64,64]{0,2,1:T(8,128)(2,1)}, bf16[1024,64,64]{0,2,1:T(8,128)(2,1)}) fusion(bf16[1024,64]{0,1:T(8,128)(2,1)S(1)} %get-tuple-element.163, bf16[1024,64]{0,1:T(8,128)(2,1)S(1)} %copy.101, bf16[1024,64]{0,1:T(8,128)(2,1)S(1)} %get-tuple-element.164), kind=kLoop, calls=%fused_computation.2.clone.1 | loop fusion | flops 8388608 | bytes 17170432 | tf_op jit(solution)/shard_map/while/body/eval_jaxpr/mul | solution.py:70
  258.7 6.2 %fusion.63 = f32[64,4096]{1,0:T(8,128)S(1)} fusion(bf16[1024,4096]{0,1:T(8,128)(2,1)} %bitcast.128, f32[1024]{0:T(1024)S(1)} %get-tuple-element.168, f32[1024]{0:T(1024)S(1)} %div.17, s32[1024]{0:T(1024)S(1)} %broadcast_add_fusion.5, f32[1024]{0:T(1024)S(1)} %get-tuple-element.170, s32[1024]{0:T(1024)S(1)} %eq.159), kind=kOutput, calls=%fused_computation.10.clone.1 | convolution fusion | flops 537329664 | bytes 9457664 | tf_op jit(solution)/shard_map/while/body/eval_jaxpr/dot_general | solution.py:71
  270.8 6.9 %broadcast_multiply_fusion.3 = (bf16[1024,64,64]{0,2,1:T(8,128)(2,1)}, bf16[1024,64,64]{0,2,1:T(8,128)(2,1)}) fusion(bf16[1024,64]{0,1:T(8,128)(2,1)S(1)} %get-tuple-element.163, bf16[1024,64]{0,1:T(8,128)(2,1)S(1)} %copy.101, bf16[1024,64]{0,1:T(8,128)(2,1)S(1)} %get-tuple-element.164), kind=kLoop, calls=%fused_computation.2.clone.1 | loop fusion | flops 8388608 | bytes 17170432 | tf_op jit(solution)/shard_map/while/body/eval_jaxpr/mul | solution.py:70
  277.9 6.2 %fusion.63 = f32[64,4096]{1,0:T(8,128)S(1)} fusion(bf16[1024,4096]{0,1:T(8,128)(2,1)} %bitcast.128, f32[1024]{0:T(1024)S(1)} %get-tuple-element.168, f32[1024]{0:T(1024)S(1)} %div.17, s32[1024]{0:T(1024)S(1)} %broadcast_add_fusion.5, f32[1024]{0:T(1024)S(1)} %get-tuple-element.170, s32[1024]{0:T(1024)S(1)} %eq.159), kind=kOutput, calls=%fused_computation.10.clone.1 | convolution fusion | flops 537329664 | bytes 9457664 | tf_op jit(solution)/shard_map/while/body/eval_jaxpr/dot_general | solution.py:71
  303.0 20.1 %collective-permute-done.9 = bf16[8]{0:T(256)(128)(2,1)S(1)} collective-permute-done((bf16[8]{0:T(256)(128)(2,1)S(1)}, bf16[8]{0:T(256)(128)(2,1)S(1)}, u32[]{:S(2)}, u32[]{:S(2)}) %collective-permute-start.9) | collective-permute-done | bytes 48 | tf_op jit(solution)/shard_map/ppermute | solution.py:23
  331.0 67.2 %collective-permute-done.12 = f32[8,32,2048]{2,1,0:T(8,128)S(1)} collective-permute-done((f32[8,32,2048]{2,1,0:T(8,128)S(1)}, f32[8,32,2048]{2,1,0:T(8,128)S(1)}, u32[]{:S(2)}, u32[]{:S(2)}) %collective-permute-start.12) | collective-permute-done | bytes 2097184 | tf_op jit(solution)/shard_map/ppermute | solution.py:23
  (234 shorter events, 139.6 us)
Async XLA Ops:
  0.0 9.2 %copy-start.3 = (bf16[8,32,2048]{2,1,0:T(8,128)(2,1)S(1)}, bf16[8,32,2048]{2,1,0:T(8,128)(2,1)}, u32[]{:S(2)}) copy-start(bf16[8,32,2048]{2,1,0:T(8,128)(2,1)} %param.10) | copy-start | bytes 3145732
  3.4 42.3 %copy-start.1 = (bf16[8,32,32,64]{3,2,1,0:T(8,128)(2,1)}, bf16[8,32,32,64]{3,2,1,0:T(8,128)(2,1)S(1)}, u32[]{:S(2)}) copy-start(bf16[8,32,32,64]{3,2,1,0:T(8,128)(2,1)S(1)} %reshape.148) | copy-start | bytes 3145732
  3.5 8.8 %collective-permute-start = (bf16[8,1,32,64]{3,2,1,0:T(8,128)(2,1)S(1)}, bf16[8,1,32,64]{3,2,1,0:T(8,128)(2,1)S(1)}, u32[]{:S(2)}, u32[]{:S(2)}) collective-permute-start(bf16[8,1,32,64]{3,2,1,0:T(8,128)(2,1)S(1)} %get-tuple-element.92), channel_id=1, source_target_pairs={{0,8},{8,16},{16,24},{1,9},{9,17},{17,25},{2,10},{10,18},{18,26},{... | collective-permute-start | bytes 98312 | tf_op jit(solution)/shard_map/ppermute | solution.py:14
  7.3 5.6 %collective-permute-start.1 = (bf16[8,1,32,64]{3,2,1,0:T(8,128)(2,1)S(1)}, bf16[8,1,32,64]{3,2,1,0:T(8,128)(2,1)S(1)}, u32[]{:S(2)}, u32[]{:S(2)}) collective-permute-start(bf16[8,1,32,64]{3,2,1,0:T(8,128)(2,1)S(1)} %get-tuple-element.91), channel_id=1, source_target_pairs={{8,0},{16,8},{24,16},{9,1},{17,9},{25,17},{10,2},{18,10},{26,18},{... | collective-permute-start | bytes 98312 | tf_op jit(solution)/shard_map/ppermute | solution.py:15
  12.3 11.9 %copy-start.5 = (bf16[576,64]{0,1:T(8,128)(2,1)S(1)}, bf16[576,64]{0,1:T(8,128)(2,1)}, u32[]{:S(2)}) copy-start(bf16[576,64]{0,1:T(8,128)(2,1)} %param.11) | copy-start | bytes 221188
  18.0 16.0 %collective-permute-start.2 = (bf16[8,34,1,64]{3,2,1,0:T(2,128)(2,1)}, bf16[8,34,1,64]{3,2,1,0:T(2,128)(2,1)}, u32[]{:S(2)}, u32[]{:S(2)}) collective-permute-start(bf16[8,34,1,64]{3,2,1,0:T(2,128)(2,1)} %get-tuple-element.83), channel_id=1, source_target_pairs={{1,0},{2,1},{3,2},{4,3},{5,4},{6,5},{7,6},{9,8},{10,9},{11,10},{12... | collective-permute-start | bytes 104456 | tf_op jit(solution)/shard_map/ppermute | solution.py:15
  20.1 13.8 %collective-permute-start.3 = (bf16[8,34,1,64]{3,2,1,0:T(2,128)(2,1)}, bf16[8,34,1,64]{3,2,1,0:T(2,128)(2,1)}, u32[]{:S(2)}, u32[]{:S(2)}) collective-permute-start(bf16[8,34,1,64]{3,2,1,0:T(2,128)(2,1)} %get-tuple-element.82), channel_id=1, source_target_pairs={{0,1},{1,2},{2,3},{3,4},{4,5},{5,6},{6,7},{8,9},{9,10},{10,11},{11... | collective-permute-start | bytes 104456 | tf_op jit(solution)/shard_map/ppermute | solution.py:14
  67.6 12.7 %copy-start.12 = (s32[2,8,1,1]{1,3,2,0:T(1,128)S(1)}, s32[2,8,1,1]{1,3,2,0:T(1,128)}, u32[]{:S(2)}) copy-start(s32[2,8,1,1]{1,3,2,0:T(1,128)} %param.15) | copy-start | bytes 196
  67.7 17.3 %copy-start.9 = (bf16[64,64]{0,1:T(8,128)(2,1)S(1)}, bf16[64,64]{0,1:T(8,128)(2,1)}, u32[]{:S(2)}) copy-start(bf16[64,64]{0,1:T(8,128)(2,1)} %get-tuple-element.96) | copy-start | bytes 24580
  67.7 17.4 %copy-start.8 = (bf16[64,64]{0,1:T(8,128)(2,1)S(1)}, bf16[64,64]{0,1:T(8,128)(2,1)}, u32[]{:S(2)}) copy-start(bf16[64,64]{0,1:T(8,128)(2,1)} %get-tuple-element.95) | copy-start | bytes 24580
  67.7 17.5 %copy-start.7 = (bf16[64,64]{0,1:T(8,128)(2,1)S(1)}, bf16[64,64]{0,1:T(8,128)(2,1)}, u32[]{:S(2)}) copy-start(bf16[64,64]{0,1:T(8,128)(2,1)} %get-tuple-element.94) | copy-start | bytes 24580
  67.7 17.6 %copy-start.6 = (bf16[64,64]{0,1:T(8,128)(2,1)S(1)}, bf16[64,64]{0,1:T(8,128)(2,1)}, u32[]{:S(2)}) copy-start(bf16[64,64]{0,1:T(8,128)(2,1)} %get-tuple-element.93) | copy-start | bytes 24580
  74.6 10.9 %collective-permute-start.4 = (bf16[8,1,32,64]{3,2,1,0:T(8,128)(2,1)S(1)}, bf16[8,1,32,64]{3,2,1,0:T(8,128)(2,1)S(1)}, u32[]{:S(2)}, u32[]{:S(2)}) collective-permute-start(bf16[8,1,32,64]{3,2,1,0:T(8,128)(2,1)S(1)} %get-tuple-element.86), channel_id=1, source_target_pairs={{0,8},{8,16},{16,24},{1,9},{9,17},{17,25},{2,10},{10,18},{18,26},{... | collective-permute-start | bytes 98312 | tf_op jit(solution)/shard_map/ppermute | solution.py:14
  78.2 7.3 %collective-permute-start.5 = (bf16[8,1,32,64]{3,2,1,0:T(8,128)(2,1)S(1)}, bf16[8,1,32,64]{3,2,1,0:T(8,128)(2,1)S(1)}, u32[]{:S(2)}, u32[]{:S(2)}) collective-permute-start(bf16[8,1,32,64]{3,2,1,0:T(8,128)(2,1)S(1)} %get-tuple-element.87), channel_id=1, source_target_pairs={{8,0},{16,8},{24,16},{9,1},{17,9},{25,17},{10,2},{18,10},{26,18},{... | collective-permute-start | bytes 98312 | tf_op jit(solution)/shard_map/ppermute | solution.py:15
  85.8 8.7 %collective-permute-start.6 = (bf16[8,34,1,64]{3,2,1,0:T(2,128)(2,1)S(1)}, bf16[8,34,1,64]{3,2,1,0:T(2,128)(2,1)S(1)}, u32[]{:S(2)}, u32[]{:S(2)}) collective-permute-start(bf16[8,34,1,64]{3,2,1,0:T(2,128)(2,1)S(1)} %get-tuple-element.78), channel_id=1, source_target_pairs={{1,0},{2,1},{3,2},{4,3},{5,4},{6,5},{7,6},{9,8},{10,9},{11,10},{12... | collective-permute-start | bytes 104456 | tf_op jit(solution)/shard_map/ppermute | solution.py:15
  87.8 8.1 %collective-permute-start.7 = (bf16[8,34,1,64]{3,2,1,0:T(2,128)(2,1)S(1)}, bf16[8,34,1,64]{3,2,1,0:T(2,128)(2,1)S(1)}, u32[]{:S(2)}, u32[]{:S(2)}) collective-permute-start(bf16[8,34,1,64]{3,2,1,0:T(2,128)(2,1)S(1)} %get-tuple-element.77), channel_id=1, source_target_pairs={{0,1},{1,2},{2,3},{3,4},{4,5},{5,6},{6,7},{8,9},{9,10},{10,11},{11... | collective-permute-start | bytes 104456 | tf_op jit(solution)/shard_map/ppermute | solution.py:14
  134.9 154.1 %copy-start.10 = (bf16[8]{0:T(256)(128)(2,1)S(1)}, bf16[8]{0:T(256)(128)(2,1)}, u32[]{:S(2)}) copy-start(bf16[8]{0:T(256)(128)(2,1)} %get-tuple-element.113) | copy-start | bytes 52
  135.0 154.0 %copy-start.11 = (bf16[8]{0:T(256)(128)(2,1)S(1)}, bf16[8]{0:T(256)(128)(2,1)}, u32[]{:S(2)}) copy-start(bf16[8]{0:T(256)(128)(2,1)} %get-tuple-element.114) | copy-start | bytes 52
  291.7 31.4 %collective-permute-start.10 = (bf16[2,8,32,2048]{3,2,1,0:T(8,128)(2,1)S(1)}, bf16[2,8,32,2048]{3,2,1,0:T(8,128)(2,1)S(1)}, u32[]{:S(2)}, u32[]{:S(2)}) collective-permute-start(bf16[2,8,32,2048]{3,2,1,0:T(8,128)(2,1)S(1)} %get-tuple-element.60), channel_id=1, source_target_pairs={{0,8},{8,16},{16,24},{1,9},{9,17},{17,25},{2,10},{10,18},{18,26},{... | collective-permute-start | bytes 6291464 | tf_op jit(solution)/shard_map/ppermute | solution.py:23
  295.5 27.7 %collective-permute-start.8 = (bf16[2,8,32,2048]{3,2,1,0:T(8,128)(2,1)S(1)}, bf16[2,8,32,2048]{3,2,1,0:T(8,128)(2,1)S(1)}, u32[]{:S(2)}, u32[]{:S(2)}) collective-permute-start(bf16[2,8,32,2048]{3,2,1,0:T(8,128)(2,1)S(1)} %get-tuple-element.62), channel_id=1, source_target_pairs={{8,0},{16,8},{24,16},{9,1},{17,9},{25,17},{10,2},{18,10},{26,18},{... | collective-permute-start | bytes 6291464 | tf_op jit(solution)/shard_map/ppermute | solution.py:23
  297.5 25.7 %collective-permute-start.9 = (bf16[8]{0:T(256)(128)(2,1)S(1)}, bf16[8]{0:T(256)(128)(2,1)S(1)}, u32[]{:S(2)}, u32[]{:S(2)}) collective-permute-start(bf16[8]{0:T(256)(128)(2,1)S(1)} %fusion.41), channel_id=1, source_target_pairs={{8,0},{16,8},{24,16},{9,1},{17,9},{25,17},{10,2},{18,10},{26,18},{... | collective-permute-start | bytes 56 | tf_op jit(solution)/shard_map/ppermute | solution.py:23
  299.4 23.8 %collective-permute-start.11 = (bf16[8]{0:T(256)(128)(2,1)S(1)}, bf16[8]{0:T(256)(128)(2,1)S(1)}, u32[]{:S(2)}, u32[]{:S(2)}) collective-permute-start(bf16[8]{0:T(256)(128)(2,1)S(1)} %fusion.41), channel_id=1, source_target_pairs={{0,8},{8,16},{16,24},{1,9},{9,17},{17,25},{2,10},{10,18},{18,26},{... | collective-permute-start | bytes 56 | tf_op jit(solution)/shard_map/ppermute | solution.py:23
  324.8 73.4 %collective-permute-start.12 = (f32[8,32,2048]{2,1,0:T(8,128)S(1)}, f32[8,32,2048]{2,1,0:T(8,128)S(1)}, u32[]{:S(2)}, u32[]{:S(2)}) collective-permute-start(f32[8,32,2048]{2,1,0:T(8,128)S(1)} %get-tuple-element.58), channel_id=1, source_target_pairs={{1,0},{2,1},{3,2},{4,3},{5,4},{6,5},{7,6},{9,8},{10,9},{11,10},{12... | collective-permute-start | bytes 6291464 | tf_op jit(solution)/shard_map/ppermute | solution.py:23
  328.0 72.0 %collective-permute-start.13 = (f32[8,32,2048]{2,1,0:T(8,128)S(1)}, f32[8,32,2048]{2,1,0:T(8,128)S(1)}, u32[]{:S(2)}, u32[]{:S(2)}) collective-permute-start(f32[8,32,2048]{2,1,0:T(8,128)S(1)} %get-tuple-element.59), channel_id=1, source_target_pairs={{0,1},{1,2},{2,3},{3,4},{4,5},{5,6},{6,7},{8,9},{9,10},{10,11},{11... | collective-permute-start | bytes 6291464 | tf_op jit(solution)/shard_map/ppermute | solution.py:23
  (11 other events, 68.3 us)
where the time goes:
time: 407 us; the launch traced here: 403 us
  local copies, waits for them, and re-layouts  93.7 us (23%)
  matrix products  91.9 us (23%)
  waiting for transfers between devices  91.1 us (22%)
  other arithmetic  83.6 us (21%)
  starting transfers between devices  41.2 us (10%)
    ppermute x6, waiting for transfers between devices, passed_along(): return lax.ppermute(x, axis, pairs)  89.1 us
    dot_general x16, matrix products, frame_region(): lax.dot_general(spread_weight, spread, (((0,), (0,)), ((), ())), preferre...  77.5 us
    mul x8, other arithmetic, frame_region(): onehot[:, :, None] * values[:, None, :]  55 us
    concatenate x2, local copies, waits for them, and re-layouts, conv_back(): jnp.concatenate([padded[:, 2 - shift_y:2 - shift_y + rows_out, 2 - shift_...  43.7 us
    concatenate x5, other arithmetic, extended(): x = jnp.concatenate([before, x, after], axis=dim)  19.3 us
    ppermute x6, starting transfers between devices, passed_along(): return lax.ppermute(x, axis, pairs)  17.4 us
    ppermute x4, starting transfers between devices, extended(): before = lax.ppermute(last, axis, up)  15.7 us
    dot_general x2, matrix products, conv_back(): jnp.einsum('fyxk,kc->fyxc', patches, kernel_stack, preferred_element_type...  14.4 us
  transfers between devices with their start and end apart: 14, of which 5 were waited for; matrix products, arithmetic and copies ran while one was open for 5% of the time, Pallas kernels for 0%

commit v1 on v0

v1 whole, which is shorter than its diff:
```python
import functools

import jax
import jax.numpy as jnp
from jax import lax
from jax.experimental import pallas as pl
from jax.experimental.pallas import tpu as pltpu
from jax.sharding import PartitionSpec as P

MESH = pl.DeviceIdType.MESH
ROWS = 48


def conv(lhs, b):
    y = jnp.dot(lhs, b, preferred_element_type=jnp.float32)
    return y


def kernel(
    n_row, n_col, frames,
    cot_ref, pre_ref, k2_ref, k1_ref, off_ref, frac_ref, tab_ref,
    out_ref,
    b2_ref, b1_ref, meta_scr, turn_scr,
    strips, strip_below, strip_above, halo, cot_right, cot_left, pre_right, pre_left, halo_right, halo_left,
    y_ref, hid_ref, w_ref, r_ref, pieces, below, above, to_left, to_right, from_right, from_left,
    tab_below, tab_above,
    row_send, row_recv, col_send, col_recv, tab_send, tab_recv,
    strip_send, strip_recv, side_send, side_recv,
):
    row = lax.axis_index("row")
    col = lax.axis_index("col")
    has_up, has_down = row > 0, row < n_row - 1
    has_left, has_right = col > 0, col < n_col - 1
    sides = ((has_up, {"row": row - 1}), (has_down, {"row": row + 1}),
             (has_left, {"col": col - 1}), (has_right, {"col": col + 1}))

    barrier = pltpu.get_barrier_semaphore()
    for there, who in sides:
        @pl.when(there)
        def _():
            pl.semaphore_signal(barrier, inc=1, device_id=who, device_id_type=MESH)

    wide = cot_ref.shape[2]
    f32 = lambda x: x.astype(jnp.float32)
    line16 = lax.broadcasted_iota(jnp.int32, (16, wide), 0)
    for g in range(frames // 4):
        first = jnp.zeros((16, wide), jnp.float32)
        last = jnp.zeros((16, wide), jnp.float32)
        for i in range(4):
            f = 4 * g + i
            mine = (line16 >= 4 * i) & (line16 < 4 * i + 4)
            x = jnp.where(line16 < 2, f32(cot_ref[f, 0:16]), pltpu.roll(f32(pre_ref[f, 0:16]), 2, 0))
            first = jnp.where(mine, pltpu.roll(x, 4 * i, 0) if i else x, first)
            x = jnp.where(line16 >= 14, f32(cot_ref[f, 16:32]), pltpu.roll(f32(pre_ref[f, 16:32]), 14, 0))
            last = jnp.where(mine, pltpu.roll(x, 4 * i + 4, 0) if i < 3 else x, last)
        strips[0, g] = first.astype(jnp.bfloat16)
        strips[1, g] = last.astype(jnp.bfloat16)

    pl.semaphore_wait(barrier, sum(there.astype(jnp.int32) for there, _ in sides))

    def tab_copy(d):
        return pltpu.make_async_remote_copy(
            src_ref=tab_ref, dst_ref=(tab_below, tab_above)[d],
            send_sem=tab_send.at[d], recv_sem=tab_recv.at[d],
            device_id=sides[d][1], device_id_type=MESH)

    def row_copy(d, f):
        return pltpu.make_async_remote_copy(
            src_ref=pieces.at[f, d], dst_ref=(below, above)[d].at[f],
            send_sem=row_send.at[d, f], recv_sem=row_recv.at[d, f],
            device_id=sides[d][1], device_id_type=MESH)

    def col_copy(d, f):
        return pltpu.make_async_remote_copy(
            src_ref=(to_left, to_right)[d].at[f], dst_ref=(from_right, from_left)[d].at[f],
            send_sem=col_send.at[d, f], recv_sem=col_recv.at[d, f],
            device_id=sides[2 + d][1], device_id_type=MESH)

    def strip_copy(d):
        return pltpu.make_async_remote_copy(
            src_ref=strips.at[d], dst_ref=(strip_below, strip_above)[d],
            send_sem=strip_send.at[d], recv_sem=strip_recv.at[d],
            device_id=sides[d][1], device_id_type=MESH)

    def side_copy(d, which):
        lanes = pl.ds(0, 128) if d == 0 else pl.ds(wide - 128, 128)
        dst = ((cot_right, cot_left), (pre_right, pre_left), (halo_right, halo_left))[which][d]
        return pltpu.make_async_remote_copy(
            src_ref=(cot_ref, pre_ref, halo)[which].at[:, :, lanes], dst_ref=dst,
            send_sem=side_send.at[d, which], recv_sem=side_recv.at[d, which],
            device_id=sides[2 + d][1], device_id_type=MESH)

    for d in range(2):
        @pl.when(sides[d][0])
        def _():
            strip_copy(d).start()
            tab_copy(d).start()
    for d in range(2):
        @pl.when(sides[2 + d][0])
        def _():
            side_copy(d, 0).start()
            side_copy(d, 1).start()

    for there, refs in ((has_down, (strip_below, tab_below, below)), (has_up, (strip_above, tab_above, above)),
                        (has_right, (cot_right, pre_right, halo_right, from_right)),
                        (has_left, (cot_left, pre_left, halo_left, from_left))):
        @pl.when(jnp.logical_not(there))
        def _():
            for ref in refs:
                @pl.loop(0, ref.shape[0])
                def _(f):
                    ref[f] = jnp.zeros(ref.shape[1:], ref.dtype)

    c = k1_ref.shape[1]
    for k_ref, b_ref in ((k2_ref, b2_ref), (k1_ref, b1_ref)):
        b_ref[...] = jnp.zeros(b_ref.shape, jnp.bfloat16)
        for t_y in range(3):
            for t in range(3):
                at = (3 * (2 - t_y) + 2 - t) * c
                block = jnp.transpose(f32(k_ref[at : at + c])).astype(jnp.bfloat16)
                for o in range(4):
                    b_ref[(o + t) * c : (o + t + 1) * c, (4 * t_y + o) * c : (4 * t_y + o + 1) * c] = block

    for d in range(2):
        @pl.when(sides[1 - d][0])
        def _():
            strip_copy(d).wait_recv()
    for f in range(frames):
        g, i = f // 4, f % 4
        low, high = f32(strip_below[g]), f32(strip_above[g])
        low = pltpu.roll(low, 16 - 4 * i, 0) if i else low
        high = pltpu.roll(high, 12 - 4 * i, 0) if i < 3 else high
        halo[f] = jnp.where(line16 < 4, low, jnp.where(line16 >= 12, high, 0.0)).astype(jnp.bfloat16)
    for d in range(2):
        @pl.when(sides[2 + d][0])
        def _():
            side_copy(d, 2).start()
    for d in range(2):
        @pl.when(sides[3 - d][0])
        def _():
            for which in range(3):
                side_copy(d, which).wait_recv()

    def compute(f):
        lane = lax.broadcasted_iota(jnp.int32, (32, 128), 1)
        low_half = lane < 64
        half = jnp.where(low_half, 0.0, 1.0)
        line = lax.broadcasted_iota(jnp.int32, (16, 128), 0)

        def cot_block(j):
            if j < 0:
                return jnp.concatenate([cot_left[f], halo_left[f]], axis=0)
            if j == 16:
                return jnp.concatenate([cot_right[f], halo_right[f]], axis=0)
            if j > 16:
                return jnp.zeros((ROWS, 128), jnp.bfloat16)
            return jnp.concatenate([cot_ref[f, :, 128 * j : 128 * j + 128], halo[f, :, 128 * j : 128 * j + 128]], axis=0)

        def pre_block(j):
            if j < 0:
                tile, edge = pre_left[f], halo_left[f]
            elif j == 16:
                tile, edge = pre_right[f], halo_right[f]
            elif j > 16:
                return jnp.zeros((ROWS, 128), jnp.float32)
            else:
                tile, edge = pre_ref[f, :, 128 * j : 128 * j + 128], halo[f, :, 128 * j : 128 * j + 128]
            edge = f32(edge)
            edge = jnp.where(line == 0, pltpu.roll(edge, 14, 0), jnp.where(line == 15, pltpu.roll(edge, 2, 0), 0.0))
            return jnp.concatenate([f32(tile), edge], axis=0)

        lhs = jnp.concatenate([jnp.concatenate([cot_block(2 * k - 1), cot_block(2 * k), cot_block(2 * k + 1)], axis=1)
                               for k in range(9)], axis=0)
        y_ref[...] = conv(lhs, b2_ref[...])
        for k in range(9):
            rows = slice(ROWS * k, ROWS * k + ROWS)
            h = (pltpu.roll(y_ref[rows, 0:256], 1, 0) + y_ref[rows, 256:512]
                 + pltpu.roll(y_ref[rows, 512:768], ROWS - 1, 0))
            pre = jnp.concatenate([pre_block(2 * k - 1), pre_block(2 * k), pre_block(2 * k + 1)], axis=1)
            pre = pltpu.roll(pre, 320, 1)[:, 0:256]
            hid_ref[:, 256 * k : 256 * k + 256] = jnp.where(pre > 0, h, 0.0).astype(jnp.bfloat16)
        lhs = jnp.concatenate([hid_ref[:, 256 * k : 256 * k + 384] for k in range(8)], axis=0)
        y_ref[0 : 8 * ROWS] = conv(lhs, b1_ref[...])
        four = jnp.concatenate([f32(r[d, f]) for r in (off_ref, frac_ref) for d in range(2)], axis=0)
        turn_scr[...] = jnp.transpose(four)
        place = lax.broadcasted_iota(jnp.int32, (8, 128), 1)
        parts = [turn_scr[pl.ds(i, 8, stride=4), :] for i in range(4)]
        for d in range(4):
            tile = jnp.zeros((8, 128), jnp.float32)
            for i in range(4):
                x = pltpu.roll(parts[i], (32 * (i - d)) % 128, 1) if i != d else parts[i]
                tile = jnp.where((place >= 32 * i) & (place < 32 * i + 32), x, tile)
            for j in range(8):
                meta_scr[d : d + 1, 128 * j : 128 * j + 128] = tile[j : j + 1]
        m = meta_scr[...]
        oy, ox = m[0:1], m[1:2].astype(jnp.int32)
        fy = m[2:3] / 16.0
        fx = m[3:4] / 16.0
        pixels = ox.shape[1]
        r0 = jnp.transpose(jnp.broadcast_to((ox & 3).astype(jnp.float32), (128, pixels)))
        r1 = jnp.where(r0 == 3.0, 0.0, r0 + 1.0)
        for k in range(8):
            rows = slice(ROWS * k, ROWS * k + ROWS)
            w = (pltpu.roll(y_ref[rows, 0:256], 1, 0) + y_ref[rows, 256:512]
                 + pltpu.roll(y_ref[rows, 512:768], ROWS - 1, 0))[0:32]
            w = w + cot_ref[f, :, 256 * k : 256 * k + 256].astype(jnp.float32)
            w = w.astype(jnp.bfloat16).astype(jnp.float32)
            for i in range(2):
                part = w[:, 128 * i : 128 * i + 128]
                turned = pltpu.roll(part, 64, 1)
                for e in range(2):
                    both = jnp.where(low_half, turned, part) if e else jnp.where(low_half, part, turned)
                    at = 64 * (2 * k + i) + 32 * e
                    for b, r in enumerate((r0, r1)):
                        which = r[at : at + 32] - half
                        for s in range(2):
                            r_ref[1024 * b + at : 1024 * b + at + 32, 128 * s : 128 * s + 128] = (
                                jnp.where(which == 2.0 * s, both, 0.0).astype(jnp.bfloat16))
        span = lax.broadcasted_iota(jnp.int32, (64, pixels), 0).astype(jnp.float32)
        wy = jnp.maximum(1.0 - jnp.abs(span - (oy + fy)), 0.0).astype(jnp.bfloat16)
        group = lax.broadcasted_iota(jnp.int32, (16, pixels), 0)
        wx = (jnp.where((ox >> 2) == group, 1.0 - fx, 0.0), jnp.where(((ox + 1) >> 2) == group, fx, 0.0))
        for n in range(16):
            for b in range(2):
                line = jnp.broadcast_to(wx[b][n : n + 1], (16, pixels)).astype(jnp.bfloat16)
                w_ref[64 * n : 64 * n + 64, pixels * b : pixels * b + pixels] = (
                    wy * jnp.concatenate([line] * 4, axis=0))
        region = jnp.dot(w_ref[...], r_ref[...], preferred_element_type=jnp.float32).astype(jnp.bfloat16)
        for n in range(16):
            for q in range(2):
                pieces[f, q, n // 8, :, 256 * (n % 8) : 256 * (n % 8) + 256] = (
                    region[64 * n + 32 * q : 64 * n + 32 * q + 32])

    def merge(f):
        for d in range(2):
            @pl.when(sides[1 - d][0])
            def _():
                row_copy(d, f).wait_recv()
        own, low, high = tab_ref[f], tab_below[f], tab_above[f]

        def scalars(t):
            return t[0:1, 0:1], t[1:2, 0:1], t[2:3, 0:1], t[3:4, 0:1]

        lo_r, hi_r, lo_c, hi_c = scalars(own)
        b_r, _, b_lo, b_hi = scalars(low)
        _, a_r, a_lo, a_hi = scalars(high)
        b_lo, b_hi, a_lo, a_hi = b_r * b_lo, b_r * b_hi, a_r * a_lo, a_r * a_hi
        for k in range(8):
            s = slice(256 * k, 256 * k + 256)
            o = [hi_r * f32(pieces[f, 0, q, :, s]) + lo_r * f32(pieces[f, 1, q, :, s]) for q in range(2)]
            lo = [f32(below[f, q, :, s]) for q in range(2)]
            up = [f32(above[f, q, :, s]) for q in range(2)]
            to_left[f, :, s] = (lo_c * o[0] + b_lo * lo[0] + a_lo * up[0]).astype(jnp.bfloat16)
            to_right[f, :, s] = (hi_c * o[1] + b_hi * lo[1] + a_hi * up[1]).astype(jnp.bfloat16)
            out_ref[f, :, s] = (hi_c * o[0] + b_hi * lo[0] + a_hi * up[0]
                                + lo_c * o[1] + b_lo * lo[1] + a_lo * up[1])
        for d in range(2):
            @pl.when(sides[2 + d][0])
            def _():
                col_copy(d, f).start()

    @pl.loop(0, frames + 1)
    def _(step):
        @pl.when(step < frames)
        def _():
            compute(step)
            for d in range(2):
                @pl.when(sides[d][0])
                def _():
                    row_copy(d, step).start()

        @pl.when(step == 0)
        def _():
            for d in range(2):
                @pl.when(sides[1 - d][0])
                def _():
                    tab_copy(d).wait_recv()

        @pl.when(step > 0)
        def _():
            merge(step - 1)

    @pl.loop(0, frames)
    def _(f):
        for d in range(2):
            @pl.when(sides[3 - d][0])
            def _():
                col_copy(d, f).wait_recv()
        out_ref[f] += from_right[f].astype(jnp.float32) + from_left[f].astype(jnp.float32)

    for d in range(2):
        @pl.when(sides[d][0])
        def _():
            tab_copy(d).wait_send()
            strip_copy(d).wait_send()

        @pl.when(sides[2 + d][0])
        def _():
            for which in range(3):
                side_copy(d, which).wait_send()

    @pl.loop(0, frames)
    def _(f):
        for d in range(2):
            @pl.when(sides[d][0])
            def _():
                row_copy(d, f).wait_send()

            @pl.when(sides[2 + d][0])
            def _():
                col_copy(d, f).wait_send()


def shards(cotangent, pre_act, kernel_one, kernel_two, offsets, fractions, anchors):
    frames, h, wc = cotangent.shape
    c = kernel_one.shape[1]
    w = wc // c
    n_row, n_col = lax.axis_size("row"), lax.axis_size("col")
    a = jnp.transpose(anchors[:, :, 0, 0]).astype(jnp.float32)
    zero = jnp.zeros((frames, 4), jnp.float32)
    tab = jnp.concatenate([-a[:, :1], 1.0 + a[:, :1], -a[:, 1:], 1.0 + a[:, 1:], zero], axis=1)
    tab = jnp.broadcast_to(tab[:, :, None], (frames, 8, 128))
    bf = jnp.bfloat16
    vmem = pl.BlockSpec(memory_space=pltpu.VMEM)
    dma = pltpu.SemaphoreType.DMA
    return pl.pallas_call(
        functools.partial(kernel, n_row, n_col, frames),
        out_shape=jax.ShapeDtypeStruct((frames, h, wc), jnp.float32),
        in_specs=[vmem] * 7,
        out_specs=vmem,
        scratch_shapes=[
            pltpu.VMEM((6 * c, 12 * c), bf),
            pltpu.VMEM((6 * c, 12 * c), bf),
            pltpu.VMEM((8, h * w), jnp.float32),
            pltpu.VMEM((w, 128), jnp.float32),
            pltpu.VMEM((2, frames // 4, 16, wc), bf),
            pltpu.VMEM((frames // 4, 16, wc), bf),
            pltpu.VMEM((frames // 4, 16, wc), bf),
            pltpu.VMEM((frames, 16, wc), bf),
            pltpu.VMEM((frames, h, 128), bf),
            pltpu.VMEM((frames, h, 128), bf),
            pltpu.VMEM((frames, h, 128), bf),
            pltpu.VMEM((frames, h, 128), bf),
            pltpu.VMEM((frames, 16, 128), bf),
            pltpu.VMEM((frames, 16, 128), bf),
            pltpu.VMEM((9 * ROWS, 12 * c), jnp.float32),
            pltpu.VMEM((ROWS, wc + 256), bf),
            pltpu.VMEM((h * w, 2 * h * w), bf),
            pltpu.VMEM((2 * h * w, 4 * c), bf),
            pltpu.VMEM((frames, 2, 2, h, wc), bf),
            pltpu.VMEM((frames, 2, h, wc), bf),
            pltpu.VMEM((frames, 2, h, wc), bf),
            pltpu.VMEM((frames, h, wc), bf),
            pltpu.VMEM((frames, h, wc), bf),
            pltpu.VMEM((frames, h, wc), bf),
            pltpu.VMEM((frames, h, wc), bf),
            pltpu.VMEM((frames, 8, 128), jnp.float32),
            pltpu.VMEM((frames, 8, 128), jnp.float32),
            dma((2, frames)), dma((2, frames)), dma((2, frames)), dma((2, frames)),
            dma((2,)), dma((2,)), dma((2,)), dma((2,)), dma((2, 3)), dma((2, 3)),
        ],
        compiler_params=pltpu.CompilerParams(
            collective_id=0, has_side_effects=True, vmem_limit_bytes=48 * 1024 * 1024
        ),
    )(cotangent, pre_act, kernel_two, kernel_one, offsets, fractions, tab)


def solution(mesh):
    in_specs = (
        P(None, "row", "col"),
        P(None, "row", "col"),
        P(),
        P(),
        P(None, None, "row", "col"),
        P(None, None, "row", "col"),
        P(None, None, "row", "col"),
    )
    out_specs = P(None, "row", "col")
    return jax.shard_map(shards, mesh=mesh, in_specs=in_specs, out_specs=out_specs, check_vma=False)
```

time: 407 us -> 73.6 us (0.18)
  matrix products: 91.9 us -> 0 us
  waiting for transfers between devices: 91.1 us -> 0 us
  local copies, waits for them, and re-layouts: 93.7 us -> 8.21 us
  other arithmetic: 83.6 us -> 0.69 us
  Pallas kernels: 0 us -> 64.3 us
  starting transfers between devices: 41.2 us -> 0 us
    dot_general x18 -> x0, matrix products: 91.9 us -> none  [the longest x16 77.5 us: frame_region(): lax.dot_general(spread_weight, spread, (((0,), (0,)), ((), ())), preferre...]
    ppermute x14 -> x0, waiting for transfers between devices: 91.1 us -> none  [the longest x6 89.1 us: passed_along(): return lax.ppermute(x, axis, pairs)]
    pallas_call x0 -> x1, Pallas kernels: none -> 64.3 us  [shards(): pl.pallas_call(functools.partial(kernel, n_row, n_col, frames), out_shape...]
    mul x10 -> x0, other arithmetic: 58.3 us -> none  [the longest x8 55 us: frame_region(): onehot[:, :, None] * values[:, None, :]]
    concatenate x5 -> x1, local copies, waits for them, and re-layouts: 44.8 us -> 0.08 us  [shards(): jnp.concatenate([-a[:, :1], 1.0 + a[:, :1], -a[:, 1:], 1.0 + a[:, 1:], ze...]
    ppermute x14 -> x0, starting transfers between devices: 41.2 us -> none  [the longest x6 17.4 us: passed_along(): return lax.ppermute(x, axis, pairs)]
    concatenate x5 -> x0, other arithmetic: 19.3 us -> none  [extended(): x = jnp.concatenate([before, x, after], axis=dim)]
    slice x15 -> x0, local copies, waits for them, and re-layouts: 15.4 us -> none  [the longest x2 7.73 us: conv_back(): padded[:, 2 - shift_y:2 - shift_y + rows_out, 2 - shift_x:2 - shift_x + c...]
  transfers between devices with their start and end apart: 14 -> 0, of which waited for: 5 -> 0; matrix products, arithmetic and copies ran while one was open for 5% -> 0% of each run, Pallas kernels for 0% -> 0%
where the time goes in v1:
time: 73.6 us; the launch traced here: 73.3 us
  Pallas kernels  64.3 us (87%)
  local copies, waits for them, and re-layouts  8.21 us (11%)
    pallas_call x1, Pallas kernels, shards(): pl.pallas_call(functools.partial(kernel, n_row, n_col, frames), out_shape...  64.3 us
    unnamed x11, local copies, waits for them, and re-layouts  7.73 us

profile of v1, /device:TPU:19, one launch (start us, length us, event | category | flops | bytes accessed | tf_op | source)
XLA Modules:
  0.0 73.3 jit_solution(12672425313249878329)
XLA Ops:
  0.0 0.7 convert_element_type.9
  0.7 0.1 copy.11
  0.8 0.1 copy.9
  0.9 0.1 copy.10
  0.9 0.1 copy.8
  1.0 0.1 concatenate.3
  1.1 0.1 broadcast_in_dim.10.tab_ref
  1.2 1.0 %copy.13.k1_ref = bf16[576,64]{1,0:T(8,128)(2,1)S(1)} copy(bf16[576,64]{0,1:T(8,128)(2,1)} %param.9) | data formatting | bytes 147456 | tf_op args[2]
  2.2 1.0 %copy.12.k2_ref = bf16[576,64]{1,0:T(8,128)(2,1)S(1)} copy(bf16[576,64]{0,1:T(8,128)(2,1)} %param.10) | data formatting | bytes 147456 | tf_op args[3]
  3.2 0.0 copy-start
  3.2 1.2 %copy-done = bf16[8,32,2048]{2,1,0:T(8,128)(2,1)S(1)} copy-done((bf16[8,32,2048]{2,1,0:T(8,128)(2,1)S(1)}, bf16[8,32,2048]{2,1,0:T(8,128)(2,1)}, u32[]{:S(2)}) %copy-start) | copy-done | bytes 1048600
  4.5 0.0 copy-start.1
  4.5 1.2 %copy-done.1 = bf16[8,32,2048]{2,1,0:T(8,128)(2,1)S(1)} copy-done((bf16[8,32,2048]{2,1,0:T(8,128)(2,1)S(1)}, bf16[8,32,2048]{2,1,0:T(8,128)(2,1)}, u32[]{:S(2)}) %copy-start.1) | copy-done | bytes 1048600
  5.7 0.0 copy-start.2
  5.7 0.9 %copy-done.2 = s32[2,8,32,32]{3,2,1,0:T(8,128)S(1)} copy-done((s32[2,8,32,32]{3,2,1,0:T(8,128)S(1)}, s32[2,8,32,32]{3,2,1,0:T(8,128)}, u32[]{:S(2)}) %copy-start.2) | copy-done | bytes 65560
  6.6 0.0 copy-start.3
  6.6 0.9 %copy-done.3 = s32[2,8,32,32]{3,2,1,0:T(8,128)S(1)} copy-done((s32[2,8,32,32]{3,2,1,0:T(8,128)S(1)}, s32[2,8,32,32]{3,2,1,0:T(8,128)}, u32[]{:S(2)}) %copy-start.3) | copy-done | bytes 65560
  7.6 64.3 %shard_map.73 = f32[8,32,2048]{2,1,0:T(8,128)S(1)} custom-call(bf16[8,32,2048]{2,1,0:T(8,128)(2,1)S(1)} %copy-done, bf16[8,32,2048]{2,1,0:T(8,128)(2,1)S(1)} %copy-done.1, bf16[576,64]{1,0:T(8,128)(2,1)S(1)} %copy.12.k2_ref, bf16[576,64]{1,0:T(8,128)(2,1)S(1)} %copy.13.k1_ref, s32[2,8,32,32]{3,2,1,0:T(8,128)S(1)} %copy-done.2, ...), custom_call_target="tpu_custom_call" | custom-call | tf_op jit(solution)/shard_map/pallas_call | solution.py:326
  71.9 1.3 %copy.15 = f32[8,32,2048]{2,1,0:T(8,128)} copy(f32[8,32,2048]{2,1,0:T(8,128)S(1)} %shard_map.73) | data formatting | bytes 4194304
  (2 shorter events, 0.0 us)
Async XLA Ops:
  3.2 1.2 %copy-start = (bf16[8,32,2048]{2,1,0:T(8,128)(2,1)S(1)}, bf16[8,32,2048]{2,1,0:T(8,128)(2,1)}, u32[]{:S(2)}) copy-start(bf16[8,32,2048]{2,1,0:T(8,128)(2,1)} %cot_ref.1) | copy-start | bytes 3145732
  4.5 1.2 %copy-start.1 = (bf16[8,32,2048]{2,1,0:T(8,128)(2,1)S(1)}, bf16[8,32,2048]{2,1,0:T(8,128)(2,1)}, u32[]{:S(2)}) copy-start(bf16[8,32,2048]{2,1,0:T(8,128)(2,1)} %pre_ref.1) | copy-start | bytes 3145732
  5.7 0.9 %copy-start.2 = (s32[2,8,32,32]{3,2,1,0:T(8,128)S(1)}, s32[2,8,32,32]{3,2,1,0:T(8,128)}, u32[]{:S(2)}) copy-start(s32[2,8,32,32]{3,2,1,0:T(8,128)} %off_ref.1) | copy-start | bytes 196612
  6.6 0.9 %copy-start.3 = (s32[2,8,32,32]{3,2,1,0:T(8,128)S(1)}, s32[2,8,32,32]{3,2,1,0:T(8,128)}, u32[]{:S(2)}) copy-start(s32[2,8,32,32]{3,2,1,0:T(8,128)} %frac_ref.1) | copy-start | bytes 196612

commit v2 on v1

--- a/solution.py
+++ b/solution.py
@@ -18,15 +18,20 @@
 
 def kernel(
     n_row, n_col, frames,
-    cot_ref, pre_ref, k2_ref, k1_ref, off_ref, frac_ref, tab_ref,
+    cot_in, pre_in, off_in, frac_in, k2_ref, k1_ref, tab_ref,
     out_ref,
+    cot_ref, pre_ref, off_ref, frac_ref,
     b2_ref, b1_ref, meta_scr, turn_scr,
     strips, strip_below, strip_above, halo, cot_right, cot_left, pre_right, pre_left, halo_right, halo_left,
     y_ref, hid_ref, w_ref, r_ref, pieces, below, above, to_left, to_right, from_right, from_left,
     tab_below, tab_above,
     row_send, row_recv, col_send, col_recv, tab_send, tab_recv,
-    strip_send, strip_recv, side_send, side_recv,
+    strip_send, strip_recv, side_send, side_recv, load_sem,
 ):
+    loads = [pltpu.make_async_copy(src, dst, load_sem.at[i]) for i, (src, dst) in enumerate(
+        ((cot_in, cot_ref), (pre_in, pre_ref), (off_in, off_ref), (frac_in, frac_ref)))]
+    for load in loads:
+        load.start()
     row = lax.axis_index("row")
     col = lax.axis_index("col")
     has_up, has_down = row > 0, row < n_row - 1
@@ -40,6 +45,8 @@
         def _():
             pl.semaphore_signal(barrier, inc=1, device_id=who, device_id_type=MESH)
 
+    loads[0].wait()
+    loads[1].wait()
     wide = cot_ref.shape[2]
     f32 = lambda x: x.astype(jnp.float32)
     line16 = lax.broadcasted_iota(jnp.int32, (16, wide), 0)
@@ -111,13 +118,13 @@
                 def _(f):
                     ref[f] = jnp.zeros(ref.shape[1:], ref.dtype)
 
-    c = k1_ref.shape[1]
+    c = k1_ref.shape[0]
     for k_ref, b_ref in ((k2_ref, b2_ref), (k1_ref, b1_ref)):
         b_ref[...] = jnp.zeros(b_ref.shape, jnp.bfloat16)
         for t_y in range(3):
             for t in range(3):
                 at = (3 * (2 - t_y) + 2 - t) * c
-                block = jnp.transpose(f32(k_ref[at : at + c])).astype(jnp.bfloat16)
+                block = k_ref[:, at : at + c]
                 for o in range(4):
                     b_ref[(o + t) * c : (o + t + 1) * c, (4 * t_y + o) * c : (4 * t_y + o + 1) * c] = block
 
@@ -259,6 +266,9 @@
             def _():
                 col_copy(d, f).start()
 
+    loads[2].wait()
+    loads[3].wait()
+
     @pl.loop(0, frames + 1)
     def _(step):
         @pl.when(step < frames)
@@ -326,9 +336,13 @@
     return pl.pallas_call(
         functools.partial(kernel, n_row, n_col, frames),
         out_shape=jax.ShapeDtypeStruct((frames, h, wc), jnp.float32),
-        in_specs=[vmem] * 7,
+        in_specs=[pl.BlockSpec(memory_space=pltpu.HBM)] * 4 + [vmem] * 3,
         out_specs=vmem,
         scratch_shapes=[
+            pltpu.VMEM((frames, h, wc), bf),
+            pltpu.VMEM((frames, h, wc), bf),
+            pltpu.VMEM(offsets.shape, jnp.int32),
+            pltpu.VMEM(fractions.shape, jnp.int32),
             pltpu.VMEM((6 * c, 12 * c), bf),
             pltpu.VMEM((6 * c, 12 * c), bf),
             pltpu.VMEM((8, h * w), jnp.float32),
@@ -357,12 +371,12 @@
             pltpu.VMEM((frames, 8, 128), jnp.float32),
             pltpu.VMEM((frames, 8, 128), jnp.float32),
             dma((2, frames)), dma((2, frames)), dma((2, frames)), dma((2, frames)),
-            dma((2,)), dma((2,)), dma((2,)), dma((2,)), dma((2, 3)), dma((2, 3)),
+            dma((2,)), dma((2,)), dma((2,)), dma((2,)), dma((2, 3)), dma((2, 3)), dma((4,)),
         ],
         compiler_params=pltpu.CompilerParams(
-            collective_id=0, has_side_effects=True, vmem_limit_bytes=48 * 1024 * 1024
+            collective_id=0, has_side_effects=True, vmem_limit_bytes=60 * 1024 * 1024
         ),
-    )(cotangent, pre_act, kernel_two, kernel_one, offsets, fractions, tab)
+    )(cotangent, pre_act, offsets, fractions, kernel_two.T, kernel_one.T, tab)
 
 
 def solution(mesh):

time: 73.6 us -> 71.9 us (0.977)
  local copies, waits for them, and re-layouts: 8.21 us -> 4.24 us
  Pallas kernels: 64.3 us -> 66.8 us
    unnamed x11 -> x1, local copies, waits for them, and re-layouts: 7.73 us -> 3.14 us
    pallas_call x1, Pallas kernels: 64.3 us -> 66.8 us  [shards(): pl.pallas_call(functools.partial(kernel, n_row, n_col, frames), out_shape...]
where the time goes in v2:
time: 71.9 us; the launch traced here: 71.7 us
  Pallas kernels  66.8 us (93%)
  local copies, waits for them, and re-layouts  4.24 us (6%)
    pallas_call x1, Pallas kernels, shards(): pl.pallas_call(functools.partial(kernel, n_row, n_col, frames), out_shape...  66.8 us
    unnamed x1, local copies, waits for them, and re-layouts  3.14 us

profile of v2, /device:TPU:19, one launch (start us, length us, event | category | flops | bytes accessed | tf_op | source)
XLA Modules:
  0.0 71.7 jit_solution(12681134807168428998)
XLA Ops:
  0.0 0.7 convert_element_type.9
  0.7 0.1 copy.11
  0.8 0.1 copy.9
  0.9 0.1 copy.10
  0.9 0.1 copy.8
  1.0 0.1 concatenate.3
  1.1 0.7 broadcast_in_dim.10.tab_ref
  1.8 66.8 %shard_map.73 = f32[8,32,2048]{2,1,0:T(8,128)} custom-call(bf16[8,32,2048]{2,1,0:T(8,128)(2,1)} %cot_in.1, bf16[8,32,2048]{2,1,0:T(8,128)(2,1)} %pre_in.1, s32[2,8,32,32]{3,2,1,0:T(8,128)} %off_in.1, s32[2,8,32,32]{3,2,1,0:T(8,128)} %frac_in.1, bf16[64,576]{1,0:T(8,128)(2,1)} %bitcast.5, bf16[64,576]{1,0:T(8,128)(2,1)} %bitcast.6, ...), custom_call_target="tpu_custom_call" | custom-call | tf_op jit(solution)/shard_map/pallas_call | solution.py:336
  68.6 3.1 %copy.13 = f32[8,32,2048]{2,1,0:T(8,128)} copy(f32[8,32,2048]{2,1,0:T(8,128)} %shard_map.73) | data formatting | bytes 4194304
  (2 shorter events, 0.0 us)

commit v3 on v2

--- a/solution.py
+++ b/solution.py
@@ -45,6 +45,17 @@
         def _():
             pl.semaphore_signal(barrier, inc=1, device_id=who, device_id_type=MESH)
 
+    def spread_weights(k_ref, b_ref):
+        c = k_ref.shape[0]
+        b_ref[...] = jnp.zeros(b_ref.shape, jnp.bfloat16)
+        for t_y in range(3):
+            for t in range(3):
+                at = (3 * (2 - t_y) + 2 - t) * c
+                block = k_ref[:, at : at + c]
+                for o in range(4):
+                    b_ref[(o + t) * c : (o + t + 1) * c, (4 * t_y + o) * c : (4 * t_y + o + 1) * c] = block
+
+    spread_weights(k2_ref, b2_ref)
     loads[0].wait()
     loads[1].wait()
     wide = cot_ref.shape[2]
@@ -118,15 +129,7 @@
                 def _(f):
                     ref[f] = jnp.zeros(ref.shape[1:], ref.dtype)
 
-    c = k1_ref.shape[0]
-    for k_ref, b_ref in ((k2_ref, b2_ref), (k1_ref, b1_ref)):
-        b_ref[...] = jnp.zeros(b_ref.shape, jnp.bfloat16)
-        for t_y in range(3):
-            for t in range(3):
-                at = (3 * (2 - t_y) + 2 - t) * c
-                block = k_ref[:, at : at + c]
-                for o in range(4):
-                    b_ref[(o + t) * c : (o + t + 1) * c, (4 * t_y + o) * c : (4 * t_y + o + 1) * c] = block
+    spread_weights(k1_ref, b1_ref)
 
     for d in range(2):
         @pl.when(sides[1 - d][0])

time: 71.9 us -> 71.9 us (level)
  no operation moved by 1% of the time
where the time goes in v3:
time: 71.9 us; the launch traced here: 71.7 us
  Pallas kernels  66.8 us (93%)
  local copies, waits for them, and re-layouts  4.24 us (6%)
    pallas_call x1, Pallas kernels, shards(): pl.pallas_call(functools.partial(kernel, n_row, n_col, frames), out_shape...  66.8 us
    unnamed x1, local copies, waits for them, and re-layouts  3.14 us

profile of v3, /device:TPU:19, one launch (start us, length us, event | category | flops | bytes accessed | tf_op | source)
XLA Modules:
  0.0 71.7 jit_solution(11333260582271162993)
XLA Ops:
  0.0 0.7 convert_element_type.9
  0.7 0.1 copy.11
  0.8 0.1 copy.9
  0.9 0.1 copy.10
  0.9 0.1 copy.8
  1.0 0.1 concatenate.3
  1.1 0.7 broadcast_in_dim.10.tab_ref
  1.8 66.8 %shard_map.73 = f32[8,32,2048]{2,1,0:T(8,128)} custom-call(bf16[8,32,2048]{2,1,0:T(8,128)(2,1)} %cot_in.1, bf16[8,32,2048]{2,1,0:T(8,128)(2,1)} %pre_in.1, s32[2,8,32,32]{3,2,1,0:T(8,128)} %off_in.1, s32[2,8,32,32]{3,2,1,0:T(8,128)} %frac_in.1, bf16[64,576]{1,0:T(8,128)(2,1)} %bitcast.5, bf16[64,576]{1,0:T(8,128)(2,1)} %bitcast.6, ...), custom_call_target="tpu_custom_call" | custom-call | tf_op jit(solution)/shard_map/pallas_call | solution.py:339
  68.6 3.1 %copy.13 = f32[8,32,2048]{2,1,0:T(8,128)} copy(f32[8,32,2048]{2,1,0:T(8,128)} %shard_map.73) | data formatting | bytes 4194304
  (2 shorter events, 0.0 us)
